TPU v7x, 256 devices: a whole 4x4x8 slice. The times are simulated.
256 devices in a mesh: seq: 8 (over x, core), res: 32 (over y, z).
Axes of the slice: x: 4, y: 4, z: 8, core: 2. Of those that a mesh axis runs over, the one named last changes fastest.
Arguments:
- alignment_matrix: bfloat16 [16, 4096, 256], P('seq', 'res'), may hold values from -400 to 400
- residue_pair_offset: bfloat16 [8, 4096, 4096], P(None, 'res'), may hold values from -400 to 400
- strand_block_filter: int32 [32, 32], replicated, may hold values from 0 to 1, as said below
- standardizer_gain: float32 [256], replicated, may hold values from 0.1 to 1.9
- combined_projection_matrix: bfloat16 [256, 1024], replicated, may hold values from -0.375 to 0.375
- final_projection_matrix: bfloat16 [256, 256], replicated, may hold values from -0.375 to 0.375
Outputs:
- columns: bfloat16 [4096, 16, 256], P(('res', 'seq'))
Inputs may be any that keep to these rules, and one draw needn't show every extreme that they name: strand_block_filter[a, b] is 1 where queries of residue tile a (residues a * 128 to a * 128 + 127) may attend to keys of tile b and 0 elsewhere; it is symmetric, 1 on the diagonal, and constant over each pair of chains, a chain being a run of consecutive tiles.
All inputs are finite; a program needn't handle non-finite values.
Results may differ from a plain program's by a relative error of at most 0.0085.
Values may be sent and summed in bfloat16 or wider, within the bound.
A program may use at most 128 MiB of HBM per device.

v0:
```python
import jax
import jax.numpy as jnp
from jax import lax
from jax.sharding import PartitionSpec as P


def standardize_features(values, gain):
    centered = values.astype(jnp.float32)
    row_mean = jnp.mean(centered, axis=-1, keepdims=True)
    centered = centered - row_mean
    variance = jnp.mean(centered * centered, axis=-1, keepdims=True)
    return centered * lax.rsqrt(variance + 1e-05) * gain


def on_device(
    alignment_matrix,
    residue_pair_offset,
    strand_block_filter,
    standardizer_gain,
    combined_projection_matrix,
    final_projection_matrix,
):
    alignment_depth, available_alignments, feature_depth = alignment_matrix.shape
    head_count = residue_pair_offset.shape[0]
    head_size = feature_depth // head_count
    standardized_alignment = standardize_features(alignment_matrix, standardizer_gain).astype(
        jnp.bfloat16
    )
    flat_rows = standardized_alignment.reshape(
        alignment_depth * available_alignments, feature_depth
    )
    tile_row = lax.dynamic_index_in_dim(
        strand_block_filter, lax.axis_index("res"), 0, keepdims=False
    )
    tile_ids = jnp.arange(tile_row.shape[0], dtype=jnp.int32)
    projected = jnp.dot(flat_rows, combined_projection_matrix, preferred_element_type=jnp.float32)
    query_part = projected[:, :feature_depth]
    gate_logit = projected[:, 3 * feature_depth :]
    own_keys = (
        projected[:, feature_depth : 2 * feature_depth]
        .astype(jnp.bfloat16)
        .reshape(alignment_depth, available_alignments, feature_depth)
    )
    own_values = (
        projected[:, 2 * feature_depth : 3 * feature_depth]
        .astype(jnp.bfloat16)
        .reshape(alignment_depth, available_alignments, feature_depth)
    )
    queries = (
        (query_part * head_size ** (-0.5))
        .astype(jnp.bfloat16)
        .reshape(alignment_depth, available_alignments, head_count, head_size)
    )

    def attend(running, key_block, value_block, offset, allowed):
        piece_len = key_block.shape[1]
        key_heads = key_block.reshape(alignment_depth, piece_len, head_count, head_size)
        value_heads = value_block.reshape(alignment_depth, piece_len, head_count, head_size)
        bias_piece = lax.dynamic_slice_in_dim(residue_pair_offset, offset, piece_len, 2)
        scores = jnp.einsum(
            "sihd,sjhd->shij", queries, key_heads, preferred_element_type=jnp.float32
        )
        scores = scores + bias_piece[None].astype(jnp.float32)
        old_max, old_total, old_sum = running
        new_max = jnp.maximum(old_max, jnp.max(jnp.where(allowed, scores, -1e30), axis=-1))
        weights = jnp.where(allowed, jnp.exp(scores - new_max[..., None]), 0.0)
        factor = jnp.exp(old_max - new_max)
        new_total = old_total * factor + jnp.sum(weights, axis=-1)
        product = jnp.einsum(
            "shij,sjhd->shid",
            weights.astype(jnp.bfloat16),
            value_heads,
            preferred_element_type=jnp.float32,
        )
        new_sum = old_sum * factor[..., None] + product
        return (new_max, new_total, new_sum)

    def visit(running, pieces, offset, prepare):
        piece_len = pieces[0].shape[1]
        block_len = 512
        for block_start in range(0, piece_len, block_len):
            segment = tuple((piece[:, block_start : block_start + block_len] for piece in pieces))
            here = offset + block_start
            key_tiles = (here + jnp.arange(block_len, dtype=jnp.int32)) // available_alignments
            allowed = (
                jnp.sum(
                    jnp.where(key_tiles[:, None] == tile_ids[None, :], tile_row[None, :], 0), axis=1
                )
                > 0
            )
            key_block, value_block = prepare(segment)
            running = attend(running, key_block, value_block, here, allowed)
        return running

    initial = (
        jnp.full((alignment_depth, head_count, available_alignments), -1e30, jnp.float32),
        jnp.zeros((alignment_depth, head_count, available_alignments), jnp.float32),
        jnp.zeros((alignment_depth, head_count, available_alignments, head_size), jnp.float32),
    )

    def fold_pairs(running, pieces, offset):
        return visit(running, pieces, offset, lambda segment: segment)

    final = fold_pairs(
        initial,
        (
            lax.all_gather(own_keys, "res", axis=1, tiled=True),
            lax.all_gather(own_values, "res", axis=1, tiled=True),
        ),
        jnp.int32(0),
    )
    attended = jnp.transpose(final[2] / final[1][..., None], (0, 2, 1, 3)).reshape(
        alignment_depth, available_alignments, feature_depth
    )
    gated = (
        jax.nn.sigmoid(gate_logit.reshape(alignment_depth, available_alignments, feature_depth))
        * attended
    ).astype(jnp.bfloat16)
    update = jnp.einsum(
        "sic,ce->ise", gated, final_projection_matrix, preferred_element_type=jnp.float32
    ).astype(jnp.bfloat16)
    return lax.all_to_all(update, "seq", split_axis=0, concat_axis=1, tiled=True)


def solution(mesh):
    return jax.shard_map(
        on_device,
        mesh=mesh,
        in_specs=(P("seq", "res", None), P(None, "res", None), P(), P(), P(), P()),
        out_specs=P(("res", "seq"), None, None),
        check_vma=False,
    )
```

profile of v0, /device:TPU:1, one launch (start us, length us, event | category | flops | bytes accessed | tf_op | source)
XLA Modules:
  0.0 274.4 jit_solution(7043988862262977643)
XLA Ops:
  12.9 9.1 %slice_convert_fusion.5 = (f32[8,128,512]{2,1,0:T(8,128)}, f32[8,128,512]{2,1,0:T(8,128)}, f32[8,128,512]{2,1,0:T(8,128)}, f32[8,128,512]{2,1,0:T(8,128)}, f32[8...) fusion(bf16[8,128,4096]{2,1,0:T(8,128)(2,1)} %param.7), kind=kLoop, calls=%fused_computation.79 | loop fusion | flops 4194304 | bytes 25165824 | tf_op jit(solution)/shard_map/convert_element_type | solution.py:63
  22.0 72.0 %all-gather.5.cloned.1.call-done = bf16[2,4096,256]{2,1,0:T(8,128)(2,1)} async-done(((bf16[2,128,256]{2,1,0:T(8,128)(2,1)}), bf16[2,4096,256]{2,1,0:T(8,128)(2,1)}) %all-gather.5.cloned.1.call-update) | async-done | bytes 4194320 | tf_op jit(solution)/shard_map/all_gather | solution.py:108
  94.0 4.2 %fusion.186 = (bf16[2,512,256]{2,1,0:T(8,128)(2,1)}, bf16[2,512,256]{2,1,0:T(8,128)(2,1)}, bf16[2,512,256]{2,1,0:T(8,128)(2,1)}, bf16[2,512,256]{2,1,0:T(8,128)(...) fusion(bf16[2,4096,256]{2,1,0:T(8,128)(2,1)} %all-gather.5.clon, ...), kind=kLoop, calls=%fused_computation.254 | loop fusion | bytes 8388608 | tf_op jit(solution)/shard_map/slice | solution.py:82
  99.4 76.2 %all-gather.3.cloned.1.call-done = bf16[2,4096,256]{2,1,0:T(8,128)(2,1)} async-done(((bf16[2,128,256]{2,1,0:T(8,128)(2,1)}), bf16[2,4096,256]{2,1,0:T(8,128)(2,1)}) %all-gather.3.cloned.1.call-update) | async-done | bytes 4194320 | tf_op jit(solution)/shard_map/all_gather | solution.py:107
  175.7 4.2 %fusion.187 = (bf16[2,512,256]{2,1,0:T(8,128)(2,1)}, bf16[2,512,256]{2,1,0:T(8,128)(2,1)}, bf16[2,512,256]{2,1,0:T(8,128)(2,1)}, bf16[2,512,256]{2,1,0:T(8,128)(...) fusion(bf16[2,4096,256]{2,1,0:T(8,128)(2,1)} %all-gather.3.clon, ...), kind=kLoop, calls=%fused_computation.255 | loop fusion | bytes 8388608 | tf_op jit(solution)/shard_map/slice | solution.py:82
  181.9 2.0 copy.110
  183.9 2.1 copy.107
  186.0 2.1 copy.104
  188.1 2.1 copy.101
  190.1 2.1 copy.98
  192.2 2.1 copy.95
  198.3 2.1 copy.97
  200.4 2.1 copy.100
  202.5 2.1 copy.103
  204.6 2.1 copy.106
  210.8 2.7 select_reduce_fusion.7
  213.5 3.8 %select_reduce_fusion = (f32[2,8,128]{2,1,0:T(8,128)S(1)}, f32[2,8,128,512]{3,2,1,0:T(8,128)}) fusion(f32[8,128,512]{2,1,0:T(8,128)S(1)} %copy-done.11, pred[512]{0:T(512)(128)(4,1)S(1)} %broadcast_compare_fusion, bf16[2,512,8,32]{1,3,2,0:T(8,128)(2,1)} %bitcast.227, bf16[2,128,8,32]{1,0,3,2:T(2,128)(2,1)S(1)} %reshape.462), kind=kOutput, calls=%fused_computation.1 | convolution fusion | flops 70252544 | bytes 6955520 | tf_op jit(solution)/shard_map/sihd,sjhd->shij/dot_general | solution.py:60
  225.3 4.1 %fusion.12 = (f32[2,8,128]{2,1,0:T(8,128)S(1)}, f32[2,8,128]{2,1,0:T(8,128)S(1)}) fusion(f32[2,8,128,512]{3,2,1,0:T(8,128)S(1)} %get-tuple-element.65, f32[2,8,128]{2,1,0:T(8,128)S(1)} %get-tuple-element.21, f32[8,128,512]{2,1,0:T(8,128)S(1)} %get-tuple-element.36, pred[512]{0:T(512)(128)(4,1)S(1)} %broadcast_compare_fusion.2, ...), kind=kLoop, calls=%fused_computation.28 | loop fusion | flops 8384512 | bytes 12616704 | tf_op jit(solution)/shard_map/reduce_sum | solution.py:68
  229.4 2.3 fusion.8
  231.7 4.0 %fusion.4 = (f32[2,8,128]{2,1,0:T(8,128)S(1)}, f32[2,8,128]{2,1,0:T(8,128)S(1)}) fusion(f32[2,8,128,512]{3,2,1,0:T(8,128)S(1)} %get-tuple-element.73, f32[2,8,128]{2,1,0:T(8,128)S(1)} %get-tuple-element.25, f32[8,128,512]{2,1,0:T(8,128)} %get-tuple-element.29, pred[512]{0:T(512)(128)(4,1)S(1)} %broadcast_compare_fusion.4, ...), kind=kLoop, calls=%fused_computation.20 | loop fusion | flops 8384512 | bytes 12616704 | tf_op jit(solution)/shard_map/reduce_sum | solution.py:68
  235.7 3.5 %fusion = (f32[2,8,128]{2,1,0:T(8,128)S(1)}, f32[2,8,128]{2,1,0:T(8,128)S(1)}) fusion(f32[2,8,128,512]{3,2,1,0:T(8,128)S(1)} %get-tuple-element.77, f32[2,8,128]{2,1,0:T(8,128)S(1)} %get-tuple-element.59, f32[8,128,512]{2,1,0:T(8,128)} %get-tuple-element.34, pred[512]{0:T(512)(128)(4,1)S(1)} %broadcast_compare_fusion.7, ...), kind=kLoop, calls=%fused_computation.16 | loop fusion | flops 8384512 | bytes 12616704 | tf_op jit(solution)/shard_map/reduce_sum | solution.py:68
  239.2 2.7 fusion.106
  242.0 2.9 %fusion.100 = f32[2,128,8,32]{1,3,2,0:T(8,128)S(1)} fusion(f32[2,128,8,32]{1,3,2,0:T(8,128)S(1)} %fusion.106, bf16[2,512,8,32]{1,3,2,0:T(8,128)(2,1)} %bitcast.220, f32[2,8,128,512]{3,2,1,0:T(8,128)S(1)} %get-tuple-element.75, f32[2,8,128]{2,1,0:T(8,128)S(1)} %get-tuple-element.26, f32[8,128,512]{2,1,0:T(8,128)} %get-tuple-element.33, ...), kind=kOutput, calls=%fused_computation.68 | convolution fusion | flops 71434240 | bytes 7356928 | tf_op jit(solution)/shard_map/shij,sjhd->shid/dot_general | solution.py:69
  254.2 12.6 %all_to_all.18 = bf16[128,2,256]{2,1,0:T(2,128)(2,1)S(1)} all-to-all(bf16[128,2,256]{2,1,0:T(2,128)(2,1)S(1)} %copy.114), channel_id=1, replica_groups=mesh['seq'=8,'res'=32] {'seq'}, dimensions={0} | all-to-all | bytes 262144 | tf_op jit(solution)/shard_map/all_to_all | solution.py:122
  (112 shorter events, 35.5 us)
Async XLA Ops:
  6.5 3.2 %copy-start = (bf16[256,1024]{1,0:T(8,128)(2,1)S(1)}, bf16[256,1024]{1,0:T(8,128)(2,1)}, u32[]{:S(2)}) copy-start(bf16[256,1024]{1,0:T(8,128)(2,1)} %param.10) | copy-start | bytes 1572868
  6.5 87.4 %all-gather.5.cloned.1.call-start = ((), (), s32[]{:S(2)}) async-start(), calls=%async_computation.2 | async-start | bytes 4325376 | tf_op jit(solution)/shard_map/all_gather | solution.py:108
  10.8 164.8 %all-gather.3.cloned.1.call-start = ((), (), s32[]{:S(2)}) async-start(), calls=%async_computation.1 | async-start | bytes 4325376 | tf_op jit(solution)/shard_map/all_gather | solution.py:107
  210.8 2.8 %copy-start.11 = (f32[8,128,512]{2,1,0:T(8,128)S(1)}, f32[8,128,512]{2,1,0:T(8,128)}, u32[]{:S(2)}) copy-start(f32[8,128,512]{2,1,0:T(8,128)} %get-tuple-element.35) | copy-start | bytes 6291460
  213.5 3.8 %copy-start.24 = (bf16[2,512,256]{1,2,0:T(8,128)(2,1)S(1)}, bf16[2,512,256]{1,2,0:T(8,128)(2,1)}, u32[]{:S(2)}) copy-start(bf16[2,512,256]{1,2,0:T(8,128)(2,1)} %copy.107) | copy-start | bytes 1572868
  217.3 1.7 copy-start.23
  218.2 1.8 copy-start.3
  218.2 1.9 copy-start.22
  219.9 1.7 copy-start.5
  219.9 1.7 copy-start.21
  220.9 1.8 copy-start.7
  220.9 1.9 copy-start.20
  222.5 1.7 copy-start.9
  222.5 1.8 copy-start.19
  231.7 4.0 %copy-start.10 = (f32[8,128,512]{2,1,0:T(8,128)S(1)}, f32[8,128,512]{2,1,0:T(8,128)}, u32[]{:S(2)}) copy-start(f32[8,128,512]{2,1,0:T(8,128)} %get-tuple-element.33) | copy-start | bytes 6291460
  241.9 3.0 %copy-start.8 = (f32[8,128,512]{2,1,0:T(8,128)S(1)}, f32[8,128,512]{2,1,0:T(8,128)}, u32[]{:S(2)}) copy-start(f32[8,128,512]{2,1,0:T(8,128)} %get-tuple-element.29) | copy-start | bytes 6291460
  241.9 3.0 %copy-start.18 = (bf16[2,512,256]{1,2,0:T(8,128)(2,1)S(1)}, bf16[2,512,256]{1,2,0:T(8,128)(2,1)}, u32[]{:S(2)}) copy-start(bf16[2,512,256]{1,2,0:T(8,128)(2,1)} %copy.97) | copy-start | bytes 1572868
  244.9 1.7 copy-start.17
  245.9 1.8 copy-start.4
  245.9 1.9 copy-start.16
  249.8 2.8 %copy-start.13 = (f32[2,8,128,512]{3,2,1,0:T(8,128)S(1)}, f32[2,8,128,512]{3,2,1,0:T(8,128)}, u32[]{:S(2)}) copy-start(f32[2,8,128,512]{3,2,1,0:T(8,128)} %get-tuple-element.63) | copy-start | bytes 12582916
  249.8 2.9 %copy-start.25 = (bf16[2,512,256]{1,2,0:T(8,128)(2,1)S(1)}, bf16[2,512,256]{1,2,0:T(8,128)(2,1)}, u32[]{:S(2)}) copy-start(bf16[2,512,256]{1,2,0:T(8,128)(2,1)} %copy.112) | copy-start | bytes 1572868
  250.9 2.9 %copy-start.26 = (bf16[256,256]{1,0:T(8,128)(2,1)S(1)}, bf16[256,256]{1,0:T(8,128)(2,1)}, u32[]{:S(2)}) copy-start(bf16[256,256]{1,0:T(8,128)(2,1)} %param.11) | copy-start | bytes 393220
  250.9 16.7 %copy-start.1 = (bf16[256,1024]{1,0:T(8,128)(2,1)S(1)}, bf16[256,1024]{1,0:T(8,128)(2,1)}, u32[]{:S(2)}) copy-start(bf16[256,1024]{1,0:T(8,128)(2,1)} %param.10) | copy-start | bytes 1572868
  (5 other events, 7.1 us)
Sparse Core Ops, SparseCore 0:
  11.0 82.9 all-gather.4
  96.6 79.0 all-gather.2
where the time goes:
time: 276 us; the launch traced here: 274 us
  waiting for transfers between devices  149 us (54%)
  local copies, waits for them, and re-layouts  48.4 us (18%)
  other arithmetic  26.6 us (10%)
  matrix products  23.9 us (9%)
  between operations  13.9 us (5%)
  blocking collectives  12.6 us (5%)
    all_gather x1, waiting for transfers between devices, on_device(): lax.all_gather(own_keys, 'res', axis=1, tiled=True)  76.2 us
    all_gather x1, waiting for transfers between devices, on_device(): lax.all_gather(own_values, 'res', axis=1, tiled=True)  72 us
    slice x18, local copies, waits for them, and re-layouts, visit(): piece[:, block_start:block_start + block_len]  40.6 us
    reduce_sum x4, other arithmetic, attend(): new_total = old_total * factor + jnp.sum(weights, axis=-1)  13.9 us
    all_to_all x1, blocking collectives, on_device(): lax.all_to_all(update, 'seq', split_axis=0, concat_axis=1, tiled=True)  12.6 us
    dot_general x8, matrix products, attend(): jnp.einsum('sihd,sjhd->shij', queries, key_heads, preferred_element_type=...  11.8 us
    dot_general x8, matrix products, attend(): jnp.einsum('shij,sjhd->shid', weights.astype(jnp.bfloat16), value_heads,...  11.6 us
    convert_element_type x1, other arithmetic, attend(): scores = scores + bias_piece[None].astype(jnp.float32)  9.1 us
  transfers between devices with their start and end apart: 2, of which 2 were waited for; matrix products, arithmetic and copies ran while one was open for 6% of the time, Pallas kernels for 0%

commit v1 on v0

v1 whole, which is shorter than its diff:
```python
import jax
import jax.numpy as jnp
from jax import lax
from jax.experimental import pallas as pl
from jax.experimental.pallas import tpu as pltpu
from jax.sharding import PartitionSpec as P

NY, NZ = 4, 8
TILES = NY * NZ
SEQ = 8
HEADS, DH, TILE, CH = 8, 32, 128, 256
ROWS = 2 * TILE
PART_A = 96
CHUNKS = (4, 4, 4, 4, 4, 4, 4, 4)
MESH = pl.DeviceIdType.MESH
BF, F32 = jnp.bfloat16, jnp.float32
NT = (((1,), (1,)), ((), ()))

SLOTS = sorted(
    ((dy, dz) for dy in (0, 1, -1, 2) for dz in (0, 1, -1, 2, -2, 3, -3, 4)),
    key=lambda d: (abs(d[0]) + abs(d[1]), abs(d[0])),
)
INDEX = {d: k for k, d in enumerate(SLOTS)}


def parent(part, slot):
    dy, dz = SLOTS[slot]
    along_z = dz != 0 if part == 0 else dy == 0
    if along_z:
        step = 1 if dz > 0 else -1
        if dz == 4 and part == 0 and dy % 2 == 1:
            step = -1
        return ("z", step), INDEX[(dy, (dz - step + 3) % NZ - 3)]
    step = 1 if dy > 0 else -1
    if dy == 2 and dz % 2 == 1:
        step = -1
    return ("y", step), INDEX[((dy - step + 1) % NY - 1, dz)]


CHILDREN = {(part, slot): [] for part in (0, 1) for slot in range(TILES)}
for _part in (0, 1):
    for _slot in range(1, TILES):
        _way, _from = parent(_part, _slot)
        CHILDREN[_part, _from].append((_way, _slot))


def chain(part, slot):
    return 1 + max([chain(part, c) for _, c in CHILDREN[part, slot]], default=0)


for _key, _list in CHILDREN.items():
    _list.sort(key=lambda e: -chain(_key[0], e[1]))


def kernel(
    x_ref, bias_ref, filter_ref, gain_ref, w_ref, wf_ref, out_ref,
    got, raw, wk, wv_t, wg_t, wf_t, keys, vals, stat, acc, mref, scores, probs, alpha, update, landed,
    send_sem, recv_sem, bias_sem, out_send, out_recv,
):
    seq, res = lax.axis_index("seq"), lax.axis_index("res")
    y, z = res // NZ, res % NZ
    near = {
        ("z", 1): y * NZ + (z + 1) % NZ,
        ("z", -1): y * NZ + (z + NZ - 1) % NZ,
        ("y", 1): ((y + 1) % NY) * NZ + z,
        ("y", -1): ((y + NY - 1) % NY) * NZ + z,
    }
    barrier = pltpu.get_barrier_semaphore()
    for other in near.values():
        pl.semaphore_signal(barrier, inc=1, device_id=(seq, other), device_id_type=MESH)
    for k in range(1, SEQ):
        pl.semaphore_signal(barrier, inc=1, device_id=((seq + k) % SEQ, res), device_id_type=MESH)

    tile_of = [((y + NY - dy) % NY) * NZ + (z + NZ - dz) % NZ for dy, dz in SLOTS]

    def bias_copy(slot):
        columns = pl.ds(pl.multiple_of(tile_of[slot] * TILE, TILE), TILE)
        return pltpu.make_async_copy(bias_ref.at[:, :, columns], raw.at[slot], bias_sem.at[slot])

    for slot in range(TILES):
        bias_copy(slot).start()

    rows = x_ref[...].reshape(ROWS, CH).astype(F32)
    rows = rows - jnp.mean(rows, axis=-1, keepdims=True)
    variance = jnp.mean(rows * rows, axis=-1, keepdims=True)
    own = (rows * lax.rsqrt(variance + 1e-5) * gain_ref[...]).astype(BF)
    got[0] = own

    pl.semaphore_wait(barrier, 4 + SEQ - 1)
    part_rows = (pl.ds(0, PART_A), pl.ds(PART_A, ROWS - PART_A))

    def block_copy(part, source, target, way):
        return pltpu.make_async_remote_copy(
            src_ref=got.at[source, part_rows[part]],
            dst_ref=got.at[target, part_rows[part]],
            send_sem=send_sem.at[target, part],
            recv_sem=recv_sem.at[target, part],
            device_id=(seq, near[way]),
            device_id_type=MESH,
        )

    started = []

    def pass_on(part, slot):
        for way, target in CHILDREN[part, slot]:
            copy = block_copy(part, slot, target, way)
            copy.start()
            started.append(copy)

    def take(part, slot):
        way, source = parent(part, slot)
        block_copy(part, source, slot, way).wait_recv()
        pass_on(part, slot)

    pass_on(0, 0)
    pass_on(1, 0)

    for part in range(2):
        for group in range(2):
            lanes = pl.ds(CH + 128 * group, 128)
            w = w_ref[:, lanes]
            if part == 1:
                w = pltpu.roll(w.astype(F32), DH, 1).astype(BF)
            wk[part, :, 128 * group : 128 * group + 128] = w
    wv_t[...] = w_ref[:, 2 * CH : 3 * CH].T
    wg_t[...] = w_ref[:, 3 * CH :].T
    wf_t[...] = wf_ref[...].T
    queries = lax.dot_general(w_ref[:, :CH].T, own, NT, preferred_element_type=F32)
    queries = (queries * DH**-0.5).astype(BF)
    unit = lax.broadcasted_iota(jnp.int32, (TILE, ROWS), 0) == lax.rem(
        lax.broadcasted_iota(jnp.int32, (TILE, ROWS), 1), TILE
    )
    unit = unit.astype(F32).astype(BF)
    for h in range(HEADS):
        first, second = DH * (h % 4), DH * ((h + 1) % 4)
        stat[h, 0:TILE, :] = jnp.zeros((TILE, ROWS), BF)
        stat[h, TILE:, :] = unit
        stat[h, first : first + DH, 0:TILE] = queries[DH * h : DH * h + DH, 0:TILE]
        stat[h, second : second + DH, TILE:] = queries[DH * h : DH * h + DH, TILE:]
        vals[h, 2 * DH :, :] = jnp.ones((16, vals.shape[2]), BF)
    acc[...] = jnp.zeros_like(acc)
    mref[...] = jnp.full(mref.shape, -1e30, F32)

    start = 0
    for index, tiles in enumerate(CHUNKS):
        if index == 0:
            for slot in range(1, tiles):
                take(0, slot)
                take(1, slot)
        size = tiles * TILE
        following = CHUNKS[index + 1] if index + 1 < len(CHUNKS) else 0
        events = [(p, s) for s in range(start + tiles, start + tiles + following) for p in (0, 1)]
        for slot in range(start, start + tiles):
            bias_copy(slot).wait()
        lane = lax.broadcasted_iota(jnp.int32, (size, 128), 1) // DH
        values = []
        for part in range(2):
            block = got[start : start + tiles, TILE * part : TILE * part + TILE].reshape(size, CH)
            keys[part, 0:size] = jnp.dot(block, wk[part], preferred_element_type=F32).astype(BF)
            values.append(
                lax.dot_general(wv_t[...], block, NT, preferred_element_type=F32).astype(BF)
            )
        for h in range(HEADS):
            for part in range(2):
                vals[h, DH * part : DH * part + DH, 0:size] = values[part][DH * h : DH * h + DH]
        closed = [
            ((1 - filter_ref[res, tile_of[slot]]).astype(F32) * -1e30).astype(BF)
            for slot in range(start, start + tiles)
        ]

        def score(h):
            lanes = slice(128 * (h // 4), 128 * (h // 4) + 128)
            key = jnp.where(lane == h % 4, keys[0, 0:size, lanes], keys[1, 0:size, lanes])
            offset = jnp.concatenate(
                [raw[start + t, h].T + closed[t] for t in range(tiles)], axis=0
            )
            scores[h % 2, 0:size] = jnp.dot(
                jnp.concatenate([key, offset], axis=1), stat[h], preferred_element_type=F32
            )

        def weigh(h):
            old = mref[h]
            new = jnp.maximum(old, jnp.max(scores[h % 2, 0:size], axis=0, keepdims=True))
            alpha[h] = jnp.exp(old - new)
            mref[h] = new
            probs[h % 2, 0:size] = jnp.exp(scores[h % 2, 0:size] - new[0:1]).astype(BF)

        def add(h):
            acc[h] = acc[h] * alpha[h, 0:1] + jnp.dot(
                vals[h, :, 0:size], probs[h % 2, 0:size], preferred_element_type=F32
            )

        for step in range(HEADS + 2):
            if step < HEADS:
                score(step)
            if 0 <= step - 1 < HEADS:
                weigh(step - 1)
            if 0 <= step - 2 < HEADS:
                add(step - 2)
            if step in EVENT_STEPS:
                k = EVENT_STEPS.index(step)
                n = len(EVENT_STEPS)
                for event in events[len(events) * k // n : len(events) * (k + 1) // n]:
                    take(*event)
        start += tiles

    gate = lax.dot_general(wg_t[...], own, NT, preferred_element_type=F32)
    attended = []
    for h in range(HEADS):
        inverse = 1.0 / acc[h, 2 * DH : 2 * DH + 1, :]
        attended.append(
            jnp.concatenate(
                [
                    acc[h, 0:DH, 0:TILE] * inverse[:, 0:TILE],
                    acc[h, DH : 2 * DH, TILE:] * inverse[:, TILE:],
                ],
                axis=1,
            )
        )
    gated = (jax.nn.sigmoid(gate) * jnp.concatenate(attended, axis=0)).astype(BF)
    new = jnp.dot(wf_t[...], gated, preferred_element_type=F32)
    update[...] = new.T.astype(BF).reshape(2, TILE, CH)

    share = TILE // SEQ

    def share_of(owner):
        return update.at[:, pl.ds(pl.multiple_of(owner * share, share), share)]

    sent = []
    for k in range(1, SEQ):
        owner = (seq + k) % SEQ
        copy = pltpu.make_async_remote_copy(
            src_ref=share_of(owner),
            dst_ref=landed.at[seq],
            send_sem=out_send.at[k],
            recv_sem=out_recv.at[k],
            device_id=(owner, res),
            device_id_type=MESH,
        )
        copy.start()
        sent.append(copy)
    mine = pltpu.make_async_copy(share_of(seq), landed.at[seq], out_recv.at[0])
    mine.start()
    for copy in started:
        copy.wait_send()
    mine.wait()
    for copy in sent:
        copy.wait()
    out_ref[...] = landed[...].reshape(2 * SEQ, share, CH)


EVENT_STEPS = (0, 1, 2, 3, 4, 5, 6, 7)


def on_device(x, bias, allowed, gain, w, wf):
    vmem = pl.BlockSpec(memory_space=pltpu.VMEM)
    longest = max(CHUNKS) * TILE
    out = pl.pallas_call(
        kernel,
        out_shape=jax.ShapeDtypeStruct((2 * SEQ, TILE // SEQ, CH), BF),
        in_specs=[
            vmem,
            pl.BlockSpec(memory_space=pl.ANY),
            pl.BlockSpec(memory_space=pltpu.SMEM),
            vmem,
            vmem,
            vmem,
        ],
        out_specs=vmem,
        scratch_shapes=[
            pltpu.VMEM((TILES, ROWS, CH), BF),
            pltpu.VMEM((TILES, HEADS, TILE, TILE), BF),
            pltpu.VMEM((2, CH, CH), BF),
            pltpu.VMEM((CH, CH), BF),
            pltpu.VMEM((CH, CH), BF),
            pltpu.VMEM((CH, CH), BF),
            pltpu.VMEM((2, longest, CH), BF),
            pltpu.VMEM((HEADS, 2 * DH + 16, longest), BF),
            pltpu.VMEM((HEADS, 2 * TILE, ROWS), BF),
            pltpu.VMEM((HEADS, 2 * DH + 16, ROWS), F32),
            pltpu.VMEM((HEADS, 8, ROWS), F32),
            pltpu.VMEM((2, longest, ROWS), F32),
            pltpu.VMEM((2, longest, ROWS), BF),
            pltpu.VMEM((HEADS, 8, ROWS), F32),
            pltpu.VMEM((2, TILE, CH), BF),
            pltpu.VMEM((SEQ, 2, TILE // SEQ, CH), BF),
            pltpu.SemaphoreType.DMA((TILES, 2)),
            pltpu.SemaphoreType.DMA((TILES, 2)),
            pltpu.SemaphoreType.DMA((TILES,)),
            pltpu.SemaphoreType.DMA((SEQ,)),
            pltpu.SemaphoreType.DMA((SEQ,)),
        ],
        compiler_params=pltpu.CompilerParams(
            collective_id=0, has_side_effects=True, vmem_limit_bytes=40 * 2**20
        ),
        cost_estimate=pl.CostEstimate(
            flops=4 * 2**30, bytes_accessed=9 * 2**20, transcendentals=2**23
        ),
    )(x, bias, allowed, gain.reshape(1, CH), w, wf)
    return jnp.transpose(out, (1, 0, 2))


def solution(mesh):
    return jax.shard_map(
        on_device,
        mesh=mesh,
        in_specs=(P("seq", "res", None), P(None, "res", None), P(), P(), P(), P()),
        out_specs=P(("res", "seq"), None, None),
        check_vma=False,
    )
```

time: 276 us -> 61.5 us (0.22)
  waiting for transfers between devices: 149 us -> 0 us
  Pallas kernels: 0 us -> 52.9 us
  local copies, waits for them, and re-layouts: 48.4 us -> 8.32 us
  other arithmetic: 26.6 us -> 0 us
  matrix products: 23.9 us -> 0 us
  between operations: 13.9 us -> 0.02 us
  blocking collectives: 12.6 us -> 0 us
    all_gather x2 -> x0, waiting for transfers between devices: 148 us -> none  [the longest x1 76.2 us: on_device(): lax.all_gather(own_keys, 'res', axis=1, tiled=True)]
    pallas_call x0 -> x1, Pallas kernels: none -> 52.9 us  [on_device(): pl.pallas_call(kernel, out_shape=jax.ShapeDtypeStruct((2 * SEQ, TILE // S...]
    slice x19 -> x0, local copies, waits for them, and re-layouts: 41.3 us -> none  [the longest x18 40.6 us: visit(): piece[:, block_start:block_start + block_len]]
    dot_general x18 -> x0, matrix products: 23.9 us -> none  [the longest x8 11.8 us: attend(): jnp.einsum('sihd,sjhd->shij', queries, key_heads, preferred_element_type=...]
    reduce_sum x7 -> x0, other arithmetic: 16.2 us -> none  [the longest x4 13.9 us: attend(): new_total = old_total * factor + jnp.sum(weights, axis=-1)]
    all_to_all x1 -> x0, blocking collectives: 12.6 us -> none  [on_device(): lax.all_to_all(update, 'seq', split_axis=0, concat_axis=1, tiled=True)]
    convert_element_type x3 -> x0, other arithmetic: 10.2 us -> none  [the longest x1 9.1 us: attend(): scores = scores + bias_piece[None].astype(jnp.float32)]
    unnamed x54 -> x12, local copies, waits for them, and re-layouts: 5.23 us -> 7.62 us
  transfers between devices with their start and end apart: 2 -> 0, of which waited for: 2 -> 0; matrix products, arithmetic and copies ran while one was open for 6% -> 0% of each run, Pallas kernels for 0% -> 0%
where the time goes in v1:
time: 61.5 us; the launch traced here: 61.3 us
  Pallas kernels  52.9 us (86%)
  local copies, waits for them, and re-layouts  8.32 us (14%)
    pallas_call x1, Pallas kernels, on_device(): pl.pallas_call(kernel, out_shape=jax.ShapeDtypeStruct((2 * SEQ, TILE // S...  52.9 us
    unnamed x12, local copies, waits for them, and re-layouts  7.62 us

profile of v1, /device:TPU:1, one launch (start us, length us, event | category | flops | bytes accessed | tf_op | source)
XLA Modules:
  0.0 61.3 jit_solution(1777886162171541672)
XLA Ops:
  0.0 0.0 copy-start
  0.0 3.4 %copy-done = bf16[8,128,4096]{2,1,0:T(8,128)(2,1)S(1)} copy-done((bf16[8,128,4096]{2,1,0:T(8,128)(2,1)S(1)}, bf16[8,128,4096]{2,1,0:T(8,128)(2,1)}, u32[]{:S(2)}) %copy-start) | copy-done | bytes 8388632
  3.4 0.0 copy-start.1
  3.4 1.0 %copy-done.1 = bf16[256,1024]{1,0:T(8,128)(2,1)S(1)} copy-done((bf16[256,1024]{1,0:T(8,128)(2,1)S(1)}, bf16[256,1024]{1,0:T(8,128)(2,1)}, u32[]{:S(2)}) %copy-start.1) | copy-done | bytes 524312
  4.4 0.0 copy-start.2
  4.4 0.9 %copy-done.2 = bf16[2,128,256]{2,1,0:T(8,128)(2,1)S(1)} copy-done((bf16[2,128,256]{2,1,0:T(8,128)(2,1)S(1)}, bf16[2,128,256]{2,1,0:T(8,128)(2,1)}, u32[]{:S(2)}) %copy-start.2) | copy-done | bytes 131096
  5.3 0.0 copy-start.3
  5.3 0.9 %copy-done.3 = bf16[256,256]{1,0:T(8,128)(2,1)S(1)} copy-done((bf16[256,256]{1,0:T(8,128)(2,1)S(1)}, bf16[256,256]{1,0:T(8,128)(2,1)}, u32[]{:S(2)}) %copy-start.3) | copy-done | bytes 131096
  6.2 0.0 copy-start.4
  6.2 0.7 %copy-done.4 = s32[32,32]{1,0:T(8,128)S(1)} copy-done((s32[32,32]{1,0:T(8,128)S(1)}, s32[32,32]{1,0:T(8,128)}, u32[]{:S(2)}) %copy-start.4) | copy-done | bytes 4120
  7.0 0.0 copy-start.5
  7.0 0.7 %copy-done.5 = f32[256]{0:T(256)S(1)} copy-done((f32[256]{0:T(256)S(1)}, f32[256]{0:T(256)}, u32[]{:S(2)}) %copy-start.5) | copy-done | bytes 1048
  7.6 52.9 %shard_map.64 = bf16[16,16,256]{2,1,0:T(8,128)(2,1)S(1)} custom-call(bf16[2,128,256]{2,1,0:T(8,128)(2,1)S(1)} %copy-done.2, bf16[8,128,4096]{2,1,0:T(8,128)(2,1)S(1)} %copy-done, s32[32,32]{1,0:T(8,128)S(1)} %copy-done.4, f32[1,256]{1,0:T(1,128)S(1)} %bitcast.3, bf16[256,1024]{1,0:T(8,128)(2,1)S(1)} %copy-done.1, bf16[256,256]{1,0:T(8,128)(2,1)S(1)} %copy-done.3), custom_call_target="tpu_custom_call" | custom-call | flops 4294967296 | bytes 9437184 | tf_op jit(solution)/shard_map/pallas_call | solution.py:258
  60.6 0.7 %copy.7 = bf16[16,16,256]{2,1,0:T(8,128)(2,1)} copy(bf16[16,16,256]{2,0,1:T(8,128)(2,1)S(1)} %bitcast.2) | data formatting | bytes 262144 | tf_op jit(solution)/shard_map/transpose | solution.py:300
Async XLA Ops:
  0.0 3.4 %copy-start = (bf16[8,128,4096]{2,1,0:T(8,128)(2,1)S(1)}, bf16[8,128,4096]{2,1,0:T(8,128)(2,1)}, u32[]{:S(2)}) copy-start(bf16[8,128,4096]{2,1,0:T(8,128)(2,1)} %bias_ref.1) | copy-start | bytes 25165828
  3.4 1.0 %copy-start.1 = (bf16[256,1024]{1,0:T(8,128)(2,1)S(1)}, bf16[256,1024]{1,0:T(8,128)(2,1)}, u32[]{:S(2)}) copy-start(bf16[256,1024]{1,0:T(8,128)(2,1)} %w_ref.1) | copy-start | bytes 1572868
  4.4 0.9 %copy-start.2 = (bf16[2,128,256]{2,1,0:T(8,128)(2,1)S(1)}, bf16[2,128,256]{2,1,0:T(8,128)(2,1)}, u32[]{:S(2)}) copy-start(bf16[2,128,256]{2,1,0:T(8,128)(2,1)} %x_ref.1) | copy-start | bytes 393220
  5.3 0.9 %copy-start.3 = (bf16[256,256]{1,0:T(8,128)(2,1)S(1)}, bf16[256,256]{1,0:T(8,128)(2,1)}, u32[]{:S(2)}) copy-start(bf16[256,256]{1,0:T(8,128)(2,1)} %wf_ref.1) | copy-start | bytes 393220
  6.2 0.7 %copy-start.4 = (s32[32,32]{1,0:T(8,128)S(1)}, s32[32,32]{1,0:T(8,128)}, u32[]{:S(2)}) copy-start(s32[32,32]{1,0:T(8,128)} %filter_ref.1) | copy-start | bytes 12292
  7.0 0.7 %copy-start.5 = (f32[256]{0:T(256)S(1)}, f32[256]{0:T(256)}, u32[]{:S(2)}) copy-start(f32[256]{0:T(256)} %param.9) | copy-start | bytes 3076

commit v2 on v1

v2 whole, which is shorter than its diff:
```python
import jax
import jax.numpy as jnp
from jax import lax
from jax.experimental import pallas as pl
from jax.experimental.pallas import tpu as pltpu
from jax.sharding import PartitionSpec as P

NY, NZ = 4, 8
TILES = NY * NZ
SEQ = 8
HEADS, DH, TILE, CH = 8, 32, 128, 256
ROWS = 2 * TILE
PARTS = (96, 80, 80)
CHUNKS = (4, 4, 4, 4, 4, 4, 4, 3, 1)
MESH = pl.DeviceIdType.MESH
BF, F32 = jnp.bfloat16, jnp.float32
NT = (((1,), (1,)), ((), ()))

SLOTS = (
    (0, 0), (1, 0), (-1, 0), (0, 1), (0, -1), (-1, -1), (-1, 1), (1, -1), (1, 1), (0, 2), (0, -2), (2, 0),
    (-1, 2), (2, -1), (-1, -2), (1, -2), (0, 3), (2, 1), (1, 2), (0, -3), (-1, 3), (2, 2), (0, 4), (2, -2),
    (1, 3), (-1, -3), (2, 3), (-1, 4), (1, 4), (1, -3), (2, -3), (2, 4),
)

SEND, TAKE, PREPARE, ATTEND = range(4)
PLAN = (
    (0, 0, 0, 1), (0, 0, 0, 2), (0, 1, 0, 3), (0, 2, 0, 4), (2,), (0, 2, 0, 1), (0, 1, 0, 2), (0, 2, 0, 3),
    (0, 1, 0, 4), (0, 1, 0, 1), (0, 2, 0, 2), (0, 0, 0, 3), (0, 0, 0, 4), (1, 1, 3), (1, 2, 4), (0, 2, 4, 7),
    (0, 1, 3, 6), (0, 1, 3, 9), (0, 2, 4, 10), (0, 1, 3, 8), (0, 2, 4, 5), (1, 0, 1), (1, 0, 2), (0, 0, 2, 6),
    (0, 0, 2, 5), (0, 0, 1, 11), (1, 2, 1), (1, 1, 2), (1, 2, 3), (1, 1, 4), (0, 1, 4, 5), (0, 2, 3, 9),
    (0, 0, 1, 7), (0, 2, 3, 6), (0, 1, 4, 7), (1, 1, 1), (1, 2, 2), (0, 0, 1, 8), (1, 0, 3), (1, 0, 4),
    (0, 1, 4, 10), (0, 2, 3, 8), (0, 2, 2, 11), (0, 0, 3, 9), (0, 0, 4, 10), (3, 0, 0, 4), (1, 2, 7),
    (1, 1, 6), (1, 1, 9), (1, 2, 10), (0, 1, 9, 12), (0, 2, 7, 13), (0, 1, 6, 17), (0, 1, 9, 16),
    (0, 2, 10, 19), (0, 1, 1, 11), (3, 0, 4, 8), (1, 1, 8), (1, 2, 5), (1, 0, 6), (1, 0, 5), (0, 0, 6, 12),
    (0, 0, 5, 14), (1, 1, 5), (1, 0, 11), (1, 2, 9), (0, 1, 5, 13), (0, 2, 9, 18), (1, 0, 7), (1, 2, 6),
    (0, 2, 9, 16), (0, 0, 7, 15), (1, 1, 7), (0, 2, 10, 15), (0, 2, 9, 12), (0, 0, 11, 17), (0, 0, 11, 13),
    (0, 1, 9, 18), (0, 2, 10, 14), (3, 1, 0, 4), (1, 0, 8), (1, 1, 10), (1, 2, 11), (1, 2, 8), (1, 0, 9),
    (1, 0, 10), (0, 1, 10, 15), (0, 1, 10, 14), (0, 0, 9, 16), (0, 1, 10, 19), (3, 1, 4, 8), (1, 1, 12),
    (1, 2, 13), (1, 1, 16), (1, 2, 19), (1, 1, 17), (1, 1, 11), (0, 2, 19, 29), (0, 1, 16, 20),
    (0, 1, 16, 22), (0, 2, 19, 22), (0, 2, 8, 17), (0, 2, 19, 25), (0, 0, 8, 18), (0, 0, 10, 19),
    (3, 2, 0, 4), (1, 0, 12), (1, 0, 14), (1, 1, 13), (1, 2, 18), (1, 2, 16), (1, 2, 12), (1, 0, 15),
    (1, 2, 15), (0, 2, 16, 20), (0, 2, 16, 24), (0, 1, 16, 24), (0, 2, 12, 21), (0, 0, 12, 20),
    (0, 0, 15, 29), (3, 2, 4, 8), (1, 2, 14), (1, 0, 17), (1, 1, 18), (1, 0, 13), (0, 0, 17, 21),
    (0, 0, 14, 25), (1, 1, 14), (1, 1, 15), (0, 1, 18, 21), (0, 2, 14, 23), (0, 0, 13, 23), (0, 1, 15, 23),
    (3, 3, 0, 4), (1, 0, 16), (1, 1, 19), (1, 1, 20), (1, 2, 29), (1, 1, 22), (1, 2, 22), (0, 1, 22, 27),
    (0, 0, 16, 22), (0, 1, 22, 28), (0, 1, 20, 26), (3, 3, 4, 8), (1, 2, 25), (1, 2, 17), (1, 0, 18),
    (1, 0, 19), (1, 2, 20), (1, 2, 24), (0, 1, 19, 25), (0, 0, 18, 24), (0, 2, 24, 26), (0, 2, 29, 30),
    (0, 2, 22, 27), (3, 4, 0, 4), (1, 0, 20), (1, 0, 29), (1, 2, 21), (1, 1, 24), (1, 0, 21), (1, 0, 25),
    (1, 2, 23), (0, 0, 21, 26), (0, 0, 25, 27), (1, 1, 21), (0, 2, 22, 28), (0, 0, 29, 28), (0, 1, 19, 29),
    (3, 4, 4, 8), (1, 1, 27), (1, 0, 22), (1, 0, 23), (1, 1, 23), (0, 0, 23, 30), (3, 5, 0, 4), (1, 1, 26),
    (1, 1, 28), (1, 0, 24), (0, 1, 28, 31), (1, 1, 25), (0, 1, 25, 30), (3, 5, 4, 8), (1, 2, 26), (1, 2, 27),
    (1, 0, 26), (1, 2, 30), (1, 0, 27), (0, 2, 27, 31), (0, 0, 26, 31), (3, 6, 0, 4), (1, 2, 28), (1, 0, 28),
    (3, 6, 4, 8), (1, 1, 29), (1, 0, 30), (1, 1, 30), (3, 7, 0, 4), (1, 1, 31), (3, 7, 4, 8), (1, 2, 31),
    (1, 0, 31), (3, 8, 0, 4), (3, 8, 4, 8),
)


def way_of(source, target):
    dy = (SLOTS[target][0] - SLOTS[source][0]) % NY
    dz = (SLOTS[target][1] - SLOTS[source][1]) % NZ
    return ("y", 1 if dy == 1 else -1) if dy else ("z", 1 if dz == 1 else -1)


FROM = {(step[1], step[3]): step[2] for step in PLAN if step[0] == SEND}


def kernel(
    x_hbm, bias_ref, filter_hbm, gain_hbm, w_hbm, wf_hbm, out_ref,
    x_ref, filter_ref, gain_ref, w_ref, wf_ref, got, raw, wk, wv_t, gate_ref, wf_t, keys, vals, stat, acc, mref, scores, probs, alpha, update, landed,
    load_sem, send_sem, recv_sem, bias_sem, out_send, out_recv,
):
    seq, res = lax.axis_index("seq"), lax.axis_index("res")
    y, z = res // NZ, res % NZ
    near = {
        ("z", 1): y * NZ + (z + 1) % NZ,
        ("z", -1): y * NZ + (z + NZ - 1) % NZ,
        ("y", 1): ((y + 1) % NY) * NZ + z,
        ("y", -1): ((y + NY - 1) % NY) * NZ + z,
    }
    loads = [
        pltpu.make_async_copy(source, target, load_sem.at[k])
        for k, (source, target) in enumerate(
            (
                (x_hbm, x_ref),
                (gain_hbm, gain_ref),
                (w_hbm, w_ref),
                (wf_hbm, wf_ref),
                (filter_hbm, filter_ref),
            )
        )
    ]
    for load in loads:
        load.start()
    barrier = pltpu.get_barrier_semaphore()
    for other in near.values():
        pl.semaphore_signal(barrier, inc=1, device_id=(seq, other), device_id_type=MESH)
    for k in range(1, SEQ):
        pl.semaphore_signal(barrier, inc=1, device_id=((seq + k) % SEQ, res), device_id_type=MESH)

    tile_of = [((y + NY - dy) % NY) * NZ + (z + NZ - dz) % NZ for dy, dz in SLOTS]

    def bias_copy(slot):
        columns = pl.ds(pl.multiple_of(tile_of[slot] * TILE, TILE), TILE)
        return pltpu.make_async_copy(bias_ref.at[:, :, columns], raw.at[slot], bias_sem.at[slot])

    for slot in range(TILES):
        bias_copy(slot).start()

    loads[0].wait()
    loads[1].wait()
    rows = x_ref[...].reshape(ROWS, CH).astype(F32)
    rows = rows - jnp.mean(rows, axis=-1, keepdims=True)
    variance = jnp.mean(rows * rows, axis=-1, keepdims=True)
    own = (rows * lax.rsqrt(variance + 1e-5) * gain_ref[...]).astype(BF)
    got[0] = own

    pl.semaphore_wait(barrier, 4 + SEQ - 1)
    part_rows = [pl.ds(sum(PARTS[:k]), PARTS[k]) for k in range(len(PARTS))]

    def block_copy(part, source, target):
        return pltpu.make_async_remote_copy(
            src_ref=got.at[source, part_rows[part]],
            dst_ref=got.at[target, part_rows[part]],
            send_sem=send_sem.at[target, part],
            recv_sem=recv_sem.at[target, part],
            device_id=(seq, near[way_of(source, target)]),
            device_id_type=MESH,
        )

    def prepare():
        for load in loads[2:]:
            load.wait()
        for part in range(2):
            for group in range(2):
                lanes = pl.ds(CH + 128 * group, 128)
                w = w_ref[:, lanes]
                if part == 1:
                    w = pltpu.roll(w.astype(F32), DH, 1).astype(BF)
                wk[part, :, 128 * group : 128 * group + 128] = w
        wv_t[...] = w_ref[:, 2 * CH : 3 * CH].T
        wf_t[...] = wf_ref[...].T
        queries = lax.dot_general(w_ref[:, :CH].T, own, NT, preferred_element_type=F32)
        queries = (queries * DH**-0.5).astype(BF)
        unit = lax.broadcasted_iota(jnp.int32, (TILE, ROWS), 0) == lax.rem(
            lax.broadcasted_iota(jnp.int32, (TILE, ROWS), 1), TILE
        )
        unit = unit.astype(F32).astype(BF)
        for h in range(HEADS):
            first, second = DH * (h % 4), DH * ((h + 1) % 4)
            stat[h, 0:TILE, :] = jnp.zeros((TILE, ROWS), BF)
            stat[h, TILE:, :] = unit
            stat[h, first : first + DH, 0:TILE] = queries[DH * h : DH * h + DH, 0:TILE]
            stat[h, second : second + DH, TILE:] = queries[DH * h : DH * h + DH, TILE:]
            for half in range(2):
                vals[half, h, 2 * DH :, :] = jnp.ones((16, vals.shape[3]), BF)
        gate_ref[...] = jax.nn.sigmoid(
            lax.dot_general(w_ref[:, 3 * CH :].T, own, NT, preferred_element_type=F32)
        )
        acc[...] = jnp.zeros_like(acc)
        mref[...] = jnp.full(mref.shape, -1e30, F32)

    first = [sum(CHUNKS[:k]) for k in range(len(CHUNKS) + 1)]

    def slots_of(chunk):
        return range(first[chunk], first[chunk + 1])

    def project_keys(chunk):
        size = CHUNKS[chunk] * TILE
        for part in range(2):
            block = got[first[chunk] : first[chunk + 1], TILE * part : TILE * part + TILE]
            block = block.reshape(size, CH)
            keys[part, 0:size] = jnp.dot(block, wk[part], preferred_element_type=F32).astype(BF)

    def project_values(chunk):
        size = CHUNKS[chunk] * TILE
        for part in range(2):
            block = got[first[chunk] : first[chunk + 1], TILE * part : TILE * part + TILE]
            block = block.reshape(size, CH)
            value = lax.dot_general(wv_t[...], block, NT, preferred_element_type=F32).astype(BF)
            for h in range(HEADS):
                vals[chunk % 2, h, DH * part : DH * part + DH, 0:size] = value[
                    DH * h : DH * h + DH
                ]

    def score(chunk, h):
        size = CHUNKS[chunk] * TILE
        lane = lax.broadcasted_iota(jnp.int32, (size, 128), 1) // DH
        lanes = slice(128 * (h // 4), 128 * (h // 4) + 128)
        key = jnp.where(lane == h % 4, keys[0, 0:size, lanes], keys[1, 0:size, lanes])
        offset = []
        for slot in slots_of(chunk):
            closed = (1 - filter_ref[res, tile_of[slot]]).astype(F32) * -1e30
            offset.append(raw[slot, h].T + closed.astype(BF))
        scores[h % 2, 0:size] = jnp.dot(
            jnp.concatenate([key, jnp.concatenate(offset, axis=0)], axis=1),
            stat[h],
            preferred_element_type=F32,
        )

    def weigh(chunk, h):
        size = CHUNKS[chunk] * TILE
        old = mref[h]
        new = jnp.maximum(old, jnp.max(scores[h % 2, 0:size], axis=0, keepdims=True))
        alpha[h] = jnp.exp(old - new)
        mref[h] = new
        probs[h % 2, 0:size] = jnp.exp(scores[h % 2, 0:size] - new[0:1]).astype(BF)

    def add(chunk, h):
        size = CHUNKS[chunk] * TILE
        acc[h] = acc[h] * alpha[h, 0:1] + jnp.dot(
            vals[chunk % 2, h, :, 0:size], probs[h % 2, 0:size], preferred_element_type=F32
        )

    work = []

    def advance(item):
        work.append(item)
        if item is not None:
            chunk, h = item
            if h == 0:
                for slot in slots_of(chunk):
                    bias_copy(slot).wait()
                project_keys(chunk)
            score(chunk, h)
            if h == 0:
                project_values(chunk)
        if len(work) > 1 and work[-2] is not None:
            weigh(*work[-2])
        if len(work) > 2:
            add(*work[-3])

    started = []
    for step in PLAN:
        if step[0] == SEND:
            copy = block_copy(*step[1:])
            copy.start()
            started.append(copy)
        elif step[0] == TAKE:
            block_copy(step[1], FROM[step[1:]], step[2]).wait_recv()
        elif step[0] == PREPARE:
            prepare()
        else:
            for h in range(step[2], step[3]):
                advance((step[1], h))
    advance(None)
    advance(None)

    attended = []
    for h in range(HEADS):
        inverse = 1.0 / acc[h, 2 * DH : 2 * DH + 1, :]
        attended.append(
            jnp.concatenate(
                [
                    acc[h, 0:DH, 0:TILE] * inverse[:, 0:TILE],
                    acc[h, DH : 2 * DH, TILE:] * inverse[:, TILE:],
                ],
                axis=1,
            )
        )
    gated = (gate_ref[...] * jnp.concatenate(attended, axis=0)).astype(BF)
    new = jnp.dot(wf_t[...], gated, preferred_element_type=F32)
    update[...] = new.T.astype(BF).reshape(2, TILE, CH)

    share = TILE // SEQ

    def share_of(owner):
        return update.at[:, pl.ds(pl.multiple_of(owner * share, share), share)]

    sent = []
    for k in range(1, SEQ):
        owner = (seq + k) % SEQ
        copy = pltpu.make_async_remote_copy(
            src_ref=share_of(owner),
            dst_ref=landed.at[seq],
            send_sem=out_send.at[k],
            recv_sem=out_recv.at[k],
            device_id=(owner, res),
            device_id_type=MESH,
        )
        copy.start()
        sent.append(copy)
    mine = pltpu.make_async_copy(share_of(seq), landed.at[seq], out_recv.at[0])
    mine.start()
    for copy in started:
        copy.wait_send()
    mine.wait()
    for copy in sent:
        copy.wait()
    out_ref[...] = landed[...].reshape(2 * SEQ, share, CH)


def on_device(x, bias, allowed, gain, w, wf):
    vmem = pl.BlockSpec(memory_space=pltpu.VMEM)
    longest = max(CHUNKS) * TILE
    out = pl.pallas_call(
        kernel,
        out_shape=jax.ShapeDtypeStruct((2 * SEQ, TILE // SEQ, CH), BF),
        in_specs=[pl.BlockSpec(memory_space=pltpu.HBM)] * 6,
        out_specs=vmem,
        scratch_shapes=[
            pltpu.VMEM((2, TILE, CH), BF),
            pltpu.SMEM((TILES, TILES), jnp.int32),
            pltpu.VMEM((1, CH), F32),
            pltpu.VMEM((CH, 4 * CH), BF),
            pltpu.VMEM((CH, CH), BF),
            pltpu.VMEM((TILES, ROWS, CH), BF),
            pltpu.VMEM((TILES, HEADS, TILE, TILE), BF),
            pltpu.VMEM((2, CH, CH), BF),
            pltpu.VMEM((CH, CH), BF),
            pltpu.VMEM((CH, ROWS), F32),
            pltpu.VMEM((CH, CH), BF),
            pltpu.VMEM((2, longest, CH), BF),
            pltpu.VMEM((2, HEADS, 2 * DH + 16, longest), BF),
            pltpu.VMEM((HEADS, 2 * TILE, ROWS), BF),
            pltpu.VMEM((HEADS, 2 * DH + 16, ROWS), F32),
            pltpu.VMEM((HEADS, 8, ROWS), F32),
            pltpu.VMEM((2, longest, ROWS), F32),
            pltpu.VMEM((2, longest, ROWS), BF),
            pltpu.VMEM((HEADS, 8, ROWS), F32),
            pltpu.VMEM((2, TILE, CH), BF),
            pltpu.VMEM((SEQ, 2, TILE // SEQ, CH), BF),
            pltpu.SemaphoreType.DMA((5,)),
            pltpu.SemaphoreType.DMA((TILES, len(PARTS))),
            pltpu.SemaphoreType.DMA((TILES, len(PARTS))),
            pltpu.SemaphoreType.DMA((TILES,)),
            pltpu.SemaphoreType.DMA((SEQ,)),
            pltpu.SemaphoreType.DMA((SEQ,)),
        ],
        compiler_params=pltpu.CompilerParams(
            collective_id=0, has_side_effects=True, vmem_limit_bytes=63 * 2**20
        ),
        cost_estimate=pl.CostEstimate(
            flops=4 * 2**30, bytes_accessed=9 * 2**20, transcendentals=2**23
        ),
    )(x, bias, allowed, gain.reshape(1, CH), w, wf)
    return jnp.transpose(out, (1, 0, 2))


def solution(mesh):
    return jax.shard_map(
        on_device,
        mesh=mesh,
        in_specs=(P("seq", "res", None), P(None, "res", None), P(), P(), P(), P()),
        out_specs=P(("res", "seq"), None, None),
        check_vma=False,
    )
```

time: 61.5 us -> 47.3 us (0.77)
  Pallas kernels: 52.9 us -> 45.6 us
  local copies, waits for them, and re-layouts: 8.32 us -> 1.6 us
    unnamed x12 -> x0, local copies, waits for them, and re-layouts: 7.62 us -> none
    pallas_call x1, Pallas kernels: 52.9 us -> 45.6 us  [on_device(): pl.pallas_call(kernel, out_shape=jax.ShapeDtypeStruct((2 * SEQ, TILE // S...]
    transpose x1, local copies, waits for them, and re-layouts: 0.7 us -> 1.6 us  [on_device(): return jnp.transpose(out, (1, 0, 2))]
where the time goes in v2:
time: 47.3 us; the launch traced here: 47.2 us
  Pallas kernels  45.6 us (96%)
  local copies, waits for them, and re-layouts  1.6 us (3%)
    pallas_call x1, Pallas kernels, on_device(): pl.pallas_call(kernel, out_shape=jax.ShapeDtypeStruct((2 * SEQ, TILE // S...  45.6 us
    transpose x1, local copies, waits for them, and re-layouts, on_device(): return jnp.transpose(out, (1, 0, 2))  1.6 us

profile of v2, /device:TPU:1, one launch (start us, length us, event | category | flops | bytes accessed | tf_op | source)
XLA Modules:
  0.0 47.2 jit_solution(5046753231400716847)
XLA Ops:
  0.0 45.6 %shard_map.64 = bf16[16,16,256]{2,1,0:T(8,128)(2,1)} custom-call(bf16[2,128,256]{2,1,0:T(8,128)(2,1)} %x_hbm.1, bf16[8,128,4096]{2,1,0:T(8,128)(2,1)} %bias_ref.1, s32[32,32]{1,0:T(8,128)} %filter_hbm.1, f32[1,256]{1,0:T(1,128)} %bitcast.3, bf16[256,1024]{1,0:T(8,128)(2,1)} %w_hbm.1, bf16[256,256]{1,0:T(8,128)(2,1)} %wf_hbm.1), custom_call_target="tpu_custom_call" | custom-call | flops 4294967296 | bytes 9437184 | tf_op jit(solution)/shard_map/pallas_call | solution.py:295
  45.6 1.6 %copy.7 = bf16[16,16,256]{2,1,0:T(8,128)(2,1)} copy(bf16[16,16,256]{2,0,1:T(8,128)(2,1)} %bitcast.2) | data formatting | bytes 262144 | tf_op jit(solution)/shard_map/transpose | solution.py:336

commit v3 on v2

--- a/solution.py
+++ b/solution.py
@@ -15,6 +15,7 @@
 MESH = pl.DeviceIdType.MESH
 BF, F32 = jnp.bfloat16, jnp.float32
 NT = (((1,), (1,)), ((), ()))
+TN = (((0,), (0,)), ((), ()))
 
 SLOTS = (
     (0, 0), (1, 0), (-1, 0), (0, 1), (0, -1), (-1, -1), (-1, 1), (1, -1), (1, 1), (0, 2), (0, -2), (2, 0),
@@ -66,7 +67,7 @@
 
 def kernel(
     x_hbm, bias_ref, filter_hbm, gain_hbm, w_hbm, wf_hbm, out_ref,
-    x_ref, filter_ref, gain_ref, w_ref, wf_ref, got, raw, wk, wv_t, gate_ref, wf_t, keys, vals, stat, acc, mref, scores, probs, alpha, update, landed,
+    x_ref, filter_ref, gain_ref, w_ref, wf_ref, got, raw, wk, wv_t, gate_ref, keys, vals, stat, acc, mref, scores, probs, alpha, update,
     load_sem, send_sem, recv_sem, bias_sem, out_send, out_recv,
 ):
     seq, res = lax.axis_index("seq"), lax.axis_index("res")
@@ -77,6 +78,12 @@
         ("y", 1): ((y + 1) % NY) * NZ + z,
         ("y", -1): ((y + NY - 1) % NY) * NZ + z,
     }
+    barrier = pltpu.get_barrier_semaphore()
+    for other in near.values():
+        pl.semaphore_signal(barrier, inc=1, device_id=(seq, other), device_id_type=MESH)
+    for k in range(1, SEQ):
+        pl.semaphore_signal(barrier, inc=1, device_id=((seq + k) % SEQ, res), device_id_type=MESH)
+
     loads = [
         pltpu.make_async_copy(source, target, load_sem.at[k])
         for k, (source, target) in enumerate(
@@ -91,20 +98,11 @@
     ]
     for load in loads:
         load.start()
-    barrier = pltpu.get_barrier_semaphore()
-    for other in near.values():
-        pl.semaphore_signal(barrier, inc=1, device_id=(seq, other), device_id_type=MESH)
-    for k in range(1, SEQ):
-        pl.semaphore_signal(barrier, inc=1, device_id=((seq + k) % SEQ, res), device_id_type=MESH)
-
     tile_of = [((y + NY - dy) % NY) * NZ + (z + NZ - dz) % NZ for dy, dz in SLOTS]
 
     def bias_copy(slot):
         columns = pl.ds(pl.multiple_of(tile_of[slot] * TILE, TILE), TILE)
         return pltpu.make_async_copy(bias_ref.at[:, :, columns], raw.at[slot], bias_sem.at[slot])
-
-    for slot in range(TILES):
-        bias_copy(slot).start()
 
     loads[0].wait()
     loads[1].wait()
@@ -128,6 +126,8 @@
         )
 
     def prepare():
+        for slot in range(TILES):
+            bias_copy(slot).start()
         for load in loads[2:]:
             load.wait()
         for part in range(2):
@@ -138,7 +138,6 @@
                     w = pltpu.roll(w.astype(F32), DH, 1).astype(BF)
                 wk[part, :, 128 * group : 128 * group + 128] = w
         wv_t[...] = w_ref[:, 2 * CH : 3 * CH].T
-        wf_t[...] = wf_ref[...].T
         queries = lax.dot_general(w_ref[:, :CH].T, own, NT, preferred_element_type=F32)
         queries = (queries * DH**-0.5).astype(BF)
         unit = lax.broadcasted_iota(jnp.int32, (TILE, ROWS), 0) == lax.rem(
@@ -258,8 +257,8 @@
             )
         )
     gated = (gate_ref[...] * jnp.concatenate(attended, axis=0)).astype(BF)
-    new = jnp.dot(wf_t[...], gated, preferred_element_type=F32)
-    update[...] = new.T.astype(BF).reshape(2, TILE, CH)
+    new = lax.dot_general(gated, wf_ref[...], TN, preferred_element_type=F32)
+    update[...] = new.astype(BF).reshape(2, TILE, CH)
 
     share = TILE // SEQ
 
@@ -267,11 +266,11 @@
         return update.at[:, pl.ds(pl.multiple_of(owner * share, share), share)]
 
     sent = []
-    for k in range(1, SEQ):
+    for k in (4, 3, 5, 2, 6, 1, 7):
         owner = (seq + k) % SEQ
         copy = pltpu.make_async_remote_copy(
             src_ref=share_of(owner),
-            dst_ref=landed.at[seq],
+            dst_ref=out_ref.at[seq],
             send_sem=out_send.at[k],
             recv_sem=out_recv.at[k],
             device_id=(owner, res),
@@ -279,24 +278,22 @@
         )
         copy.start()
         sent.append(copy)
-    mine = pltpu.make_async_copy(share_of(seq), landed.at[seq], out_recv.at[0])
+    mine = pltpu.make_async_copy(share_of(seq), out_ref.at[seq], out_recv.at[0])
     mine.start()
     for copy in started:
         copy.wait_send()
     mine.wait()
     for copy in sent:
         copy.wait()
-    out_ref[...] = landed[...].reshape(2 * SEQ, share, CH)
 
 
 def on_device(x, bias, allowed, gain, w, wf):
-    vmem = pl.BlockSpec(memory_space=pltpu.VMEM)
     longest = max(CHUNKS) * TILE
     out = pl.pallas_call(
         kernel,
-        out_shape=jax.ShapeDtypeStruct((2 * SEQ, TILE // SEQ, CH), BF),
+        out_shape=jax.ShapeDtypeStruct((SEQ, 2, TILE // SEQ, CH), BF),
         in_specs=[pl.BlockSpec(memory_space=pltpu.HBM)] * 6,
-        out_specs=vmem,
+        out_specs=pl.BlockSpec(memory_space=pltpu.HBM),
         scratch_shapes=[
             pltpu.VMEM((2, TILE, CH), BF),
             pltpu.SMEM((TILES, TILES), jnp.int32),
@@ -308,7 +305,6 @@
             pltpu.VMEM((2, CH, CH), BF),
             pltpu.VMEM((CH, CH), BF),
             pltpu.VMEM((CH, ROWS), F32),
-            pltpu.VMEM((CH, CH), BF),
             pltpu.VMEM((2, longest, CH), BF),
             pltpu.VMEM((2, HEADS, 2 * DH + 16, longest), BF),
             pltpu.VMEM((HEADS, 2 * TILE, ROWS), BF),
@@ -318,7 +314,6 @@
             pltpu.VMEM((2, longest, ROWS), BF),
             pltpu.VMEM((HEADS, 8, ROWS), F32),
             pltpu.VMEM((2, TILE, CH), BF),
-            pltpu.VMEM((SEQ, 2, TILE // SEQ, CH), BF),
             pltpu.SemaphoreType.DMA((5,)),
             pltpu.SemaphoreType.DMA((TILES, len(PARTS))),
             pltpu.SemaphoreType.DMA((TILES, len(PARTS))),
@@ -333,7 +328,7 @@
             flops=4 * 2**30, bytes_accessed=9 * 2**20, transcendentals=2**23
         ),
     )(x, bias, allowed, gain.reshape(1, CH), w, wf)
-    return jnp.transpose(out, (1, 0, 2))
+    return jnp.transpose(out.reshape(2 * SEQ, TILE // SEQ, CH), (1, 0, 2))
 
 
 def solution(mesh):

time: 47.3 us -> 46.4 us (0.981)
  Pallas kernels: 45.6 us -> 44.7 us
    transpose x1 -> x0, local copies, waits for them, and re-layouts: 1.6 us -> none  [on_device(): return jnp.transpose(out, (1, 0, 2))]
    reshape x0 -> x1, local copies, waits for them, and re-layouts: none -> 1.6 us  [on_device(): return jnp.transpose(out.reshape(2 * SEQ, TILE // SEQ, CH), (1, 0, 2))]
    pallas_call x1, Pallas kernels: 45.6 us -> 44.7 us  [on_device(): pl.pallas_call(kernel, out_shape=jax.ShapeDtypeStruct((SEQ, 2, TILE // SE...]
where the time goes in v3:
time: 46.4 us; the launch traced here: 46.3 us
  Pallas kernels  44.7 us (96%)
  local copies, waits for them, and re-layouts  1.6 us (3%)
    pallas_call x1, Pallas kernels, on_device(): pl.pallas_call(kernel, out_shape=jax.ShapeDtypeStruct((SEQ, 2, TILE // SE...  44.7 us
    reshape x1, local copies, waits for them, and re-layouts, on_device(): return jnp.transpose(out.reshape(2 * SEQ, TILE // SEQ, CH), (1, 0, 2))  1.6 us

profile of v3, /device:TPU:1, one launch (start us, length us, event | category | flops | bytes accessed | tf_op | source)
XLA Modules:
  0.0 46.3 jit_solution(4284354117807198941)
XLA Ops:
  0.0 44.7 %shard_map.64 = bf16[8,2,16,256]{3,2,1,0:T(8,128)(2,1)} custom-call(bf16[2,128,256]{2,1,0:T(8,128)(2,1)} %x_hbm.1, bf16[8,128,4096]{2,1,0:T(8,128)(2,1)} %bias_ref.1, s32[32,32]{1,0:T(8,128)} %filter_hbm.1, f32[1,256]{1,0:T(1,128)} %bitcast.6, bf16[256,1024]{1,0:T(8,128)(2,1)} %w_hbm.1, bf16[256,256]{1,0:T(8,128)(2,1)} %wf_hbm.1), custom_call_target="tpu_custom_call" | custom-call | flops 4294967296 | bytes 9437184 | tf_op jit(solution)/shard_map/pallas_call | solution.py:292
  44.7 1.6 %copy.9 = bf16[16,16,256]{2,0,1:T(8,128)(2,1)} copy(bf16[16,16,256]{2,1,0:T(8,128)(2,1)} %bitcast.5) | data formatting | bytes 262144 | tf_op jit(solution)/shard_map/reshape | solution.py:331

commit v4 on v3

--- a/solution.py
+++ b/solution.py
@@ -10,49 +10,48 @@
 SEQ = 8
 HEADS, DH, TILE, CH = 8, 32, 128, 256
 ROWS = 2 * TILE
-PARTS = (96, 80, 80)
-CHUNKS = (4, 4, 4, 4, 4, 4, 4, 3, 1)
+PARTS = (112, 80, 64)
+CHUNKS = (3, 3, 4, 3, 3, 3, 4, 3, 4, 2)
 MESH = pl.DeviceIdType.MESH
 BF, F32 = jnp.bfloat16, jnp.float32
 NT = (((1,), (1,)), ((), ()))
 TN = (((0,), (0,)), ((), ()))
 
 SLOTS = (
-    (0, 0), (1, 0), (-1, 0), (0, 1), (0, -1), (-1, -1), (-1, 1), (1, -1), (1, 1), (0, 2), (0, -2), (2, 0),
-    (-1, 2), (2, -1), (-1, -2), (1, -2), (0, 3), (2, 1), (1, 2), (0, -3), (-1, 3), (2, 2), (0, 4), (2, -2),
-    (1, 3), (-1, -3), (2, 3), (-1, 4), (1, 4), (1, -3), (2, -3), (2, 4),
+    (0, 0), (1, 0), (-1, 0), (0, 1), (0, -1), (-1, -1), (1, 1), (-1, 1), (2, 0), (0, 2), (0, -2), (-1, -2),
+    (1, -1), (2, 1), (-1, 2), (1, -2), (0, 3), (2, -1), (2, 2), (-1, -3), (0, -3), (1, 2), (1, -3), (-1, 3),
+    (2, -2), (-1, 4), (0, 4), (2, 3), (1, 4), (1, 3), (2, 4), (2, -3),
 )
 
 SEND, TAKE, PREPARE, ATTEND = range(4)
 PLAN = (
     (0, 0, 0, 1), (0, 0, 0, 2), (0, 1, 0, 3), (0, 2, 0, 4), (2,), (0, 2, 0, 1), (0, 1, 0, 2), (0, 2, 0, 3),
-    (0, 1, 0, 4), (0, 1, 0, 1), (0, 2, 0, 2), (0, 0, 0, 3), (0, 0, 0, 4), (1, 1, 3), (1, 2, 4), (0, 2, 4, 7),
-    (0, 1, 3, 6), (0, 1, 3, 9), (0, 2, 4, 10), (0, 1, 3, 8), (0, 2, 4, 5), (1, 0, 1), (1, 0, 2), (0, 0, 2, 6),
-    (0, 0, 2, 5), (0, 0, 1, 11), (1, 2, 1), (1, 1, 2), (1, 2, 3), (1, 1, 4), (0, 1, 4, 5), (0, 2, 3, 9),
-    (0, 0, 1, 7), (0, 2, 3, 6), (0, 1, 4, 7), (1, 1, 1), (1, 2, 2), (0, 0, 1, 8), (1, 0, 3), (1, 0, 4),
-    (0, 1, 4, 10), (0, 2, 3, 8), (0, 2, 2, 11), (0, 0, 3, 9), (0, 0, 4, 10), (3, 0, 0, 4), (1, 2, 7),
-    (1, 1, 6), (1, 1, 9), (1, 2, 10), (0, 1, 9, 12), (0, 2, 7, 13), (0, 1, 6, 17), (0, 1, 9, 16),
-    (0, 2, 10, 19), (0, 1, 1, 11), (3, 0, 4, 8), (1, 1, 8), (1, 2, 5), (1, 0, 6), (1, 0, 5), (0, 0, 6, 12),
-    (0, 0, 5, 14), (1, 1, 5), (1, 0, 11), (1, 2, 9), (0, 1, 5, 13), (0, 2, 9, 18), (1, 0, 7), (1, 2, 6),
-    (0, 2, 9, 16), (0, 0, 7, 15), (1, 1, 7), (0, 2, 10, 15), (0, 2, 9, 12), (0, 0, 11, 17), (0, 0, 11, 13),
-    (0, 1, 9, 18), (0, 2, 10, 14), (3, 1, 0, 4), (1, 0, 8), (1, 1, 10), (1, 2, 11), (1, 2, 8), (1, 0, 9),
-    (1, 0, 10), (0, 1, 10, 15), (0, 1, 10, 14), (0, 0, 9, 16), (0, 1, 10, 19), (3, 1, 4, 8), (1, 1, 12),
-    (1, 2, 13), (1, 1, 16), (1, 2, 19), (1, 1, 17), (1, 1, 11), (0, 2, 19, 29), (0, 1, 16, 20),
-    (0, 1, 16, 22), (0, 2, 19, 22), (0, 2, 8, 17), (0, 2, 19, 25), (0, 0, 8, 18), (0, 0, 10, 19),
-    (3, 2, 0, 4), (1, 0, 12), (1, 0, 14), (1, 1, 13), (1, 2, 18), (1, 2, 16), (1, 2, 12), (1, 0, 15),
-    (1, 2, 15), (0, 2, 16, 20), (0, 2, 16, 24), (0, 1, 16, 24), (0, 2, 12, 21), (0, 0, 12, 20),
-    (0, 0, 15, 29), (3, 2, 4, 8), (1, 2, 14), (1, 0, 17), (1, 1, 18), (1, 0, 13), (0, 0, 17, 21),
-    (0, 0, 14, 25), (1, 1, 14), (1, 1, 15), (0, 1, 18, 21), (0, 2, 14, 23), (0, 0, 13, 23), (0, 1, 15, 23),
-    (3, 3, 0, 4), (1, 0, 16), (1, 1, 19), (1, 1, 20), (1, 2, 29), (1, 1, 22), (1, 2, 22), (0, 1, 22, 27),
-    (0, 0, 16, 22), (0, 1, 22, 28), (0, 1, 20, 26), (3, 3, 4, 8), (1, 2, 25), (1, 2, 17), (1, 0, 18),
-    (1, 0, 19), (1, 2, 20), (1, 2, 24), (0, 1, 19, 25), (0, 0, 18, 24), (0, 2, 24, 26), (0, 2, 29, 30),
-    (0, 2, 22, 27), (3, 4, 0, 4), (1, 0, 20), (1, 0, 29), (1, 2, 21), (1, 1, 24), (1, 0, 21), (1, 0, 25),
-    (1, 2, 23), (0, 0, 21, 26), (0, 0, 25, 27), (1, 1, 21), (0, 2, 22, 28), (0, 0, 29, 28), (0, 1, 19, 29),
-    (3, 4, 4, 8), (1, 1, 27), (1, 0, 22), (1, 0, 23), (1, 1, 23), (0, 0, 23, 30), (3, 5, 0, 4), (1, 1, 26),
-    (1, 1, 28), (1, 0, 24), (0, 1, 28, 31), (1, 1, 25), (0, 1, 25, 30), (3, 5, 4, 8), (1, 2, 26), (1, 2, 27),
-    (1, 0, 26), (1, 2, 30), (1, 0, 27), (0, 2, 27, 31), (0, 0, 26, 31), (3, 6, 0, 4), (1, 2, 28), (1, 0, 28),
-    (3, 6, 4, 8), (1, 1, 29), (1, 0, 30), (1, 1, 30), (3, 7, 0, 4), (1, 1, 31), (3, 7, 4, 8), (1, 2, 31),
-    (1, 0, 31), (3, 8, 0, 4), (3, 8, 4, 8),
+    (0, 1, 0, 4), (0, 1, 0, 1), (0, 0, 0, 3), (0, 2, 0, 2), (0, 0, 0, 4), (1, 2, 4), (0, 2, 4, 12),
+    (0, 2, 4, 5), (0, 2, 4, 10), (1, 1, 3), (0, 1, 3, 9), (0, 1, 3, 6), (0, 1, 3, 7), (1, 0, 1), (1, 0, 2),
+    (0, 0, 2, 5), (0, 0, 1, 6), (0, 0, 1, 8), (1, 2, 1), (1, 2, 3), (0, 2, 3, 7), (1, 1, 2), (1, 1, 4),
+    (0, 1, 4, 10), (0, 2, 3, 9), (0, 1, 4, 5), (1, 1, 1), (1, 2, 2), (0, 2, 3, 6), (0, 2, 2, 8), (0, 0, 2, 7),
+    (0, 0, 1, 12), (0, 1, 1, 8), (3, 0, 0, 8), (1, 0, 3), (1, 0, 4), (1, 2, 12), (1, 2, 5), (1, 2, 10),
+    (1, 1, 9), (0, 2, 12, 17), (0, 2, 10, 11), (0, 0, 3, 9), (0, 2, 10, 20), (1, 1, 6), (1, 1, 7),
+    (0, 1, 7, 13), (0, 0, 4, 10), (0, 2, 10, 15), (1, 0, 5), (1, 0, 6), (1, 2, 7), (0, 1, 9, 16),
+    (0, 1, 9, 14), (1, 0, 8), (0, 1, 9, 21), (1, 2, 9), (1, 1, 10), (0, 0, 5, 11), (1, 1, 5), (0, 1, 10, 15),
+    (0, 1, 10, 11), (0, 0, 8, 13), (0, 1, 10, 20), (0, 1, 4, 12), (0, 2, 9, 14), (0, 2, 9, 16), (3, 1, 0, 8),
+    (1, 2, 6), (1, 2, 8), (1, 0, 7), (1, 0, 12), (1, 1, 8), (1, 2, 11), (1, 2, 20), (1, 2, 17),
+    (0, 2, 20, 19), (0, 0, 7, 14), (0, 0, 12, 15), (1, 0, 9), (0, 2, 6, 13), (0, 2, 20, 22), (0, 2, 11, 24),
+    (0, 0, 9, 16), (0, 2, 20, 26), (0, 2, 9, 21), (0, 1, 5, 17), (0, 0, 8, 17), (3, 2, 0, 8), (1, 1, 13),
+    (1, 2, 15), (1, 0, 10), (1, 1, 16), (1, 1, 14), (1, 1, 21), (1, 0, 11), (1, 1, 11), (1, 0, 13),
+    (1, 1, 15), (0, 1, 16, 29), (0, 1, 16, 23), (0, 0, 13, 18), (1, 2, 14), (1, 2, 16), (1, 1, 20),
+    (0, 2, 16, 23), (0, 1, 20, 22), (0, 0, 11, 19), (1, 1, 12), (0, 1, 21, 18), (0, 2, 14, 18),
+    (0, 1, 16, 26), (0, 0, 10, 20), (0, 1, 20, 19), (0, 0, 6, 21), (0, 2, 16, 29), (3, 3, 0, 8), (1, 2, 19),
+    (1, 2, 13), (1, 0, 14), (1, 0, 15), (1, 2, 24), (1, 2, 22), (1, 2, 26), (1, 1, 17), (1, 2, 21),
+    (0, 2, 26, 28), (0, 2, 26, 25), (0, 0, 14, 23), (0, 0, 15, 22), (0, 2, 22, 31), (3, 4, 0, 8), (1, 0, 16),
+    (1, 1, 23), (1, 1, 29), (1, 0, 17), (1, 0, 18), (1, 2, 23), (1, 1, 22), (0, 1, 15, 24), (0, 1, 23, 27),
+    (0, 0, 18, 27), (0, 0, 17, 24), (1, 0, 19), (1, 2, 18), (1, 1, 26), (0, 1, 26, 25), (1, 1, 18),
+    (0, 1, 26, 28), (0, 0, 16, 26), (0, 0, 19, 25), (3, 5, 0, 8), (1, 1, 19), (1, 2, 29), (1, 0, 20),
+    (1, 0, 21), (1, 2, 25), (1, 2, 28), (0, 2, 29, 27), (0, 1, 19, 31), (0, 0, 21, 29), (1, 0, 22),
+    (0, 0, 22, 28), (0, 2, 25, 30), (3, 6, 0, 8), (1, 0, 23), (1, 2, 31), (1, 1, 27), (1, 1, 24), (1, 0, 24),
+    (1, 0, 27), (1, 1, 25), (1, 1, 28), (0, 1, 28, 30), (0, 0, 27, 30), (0, 0, 24, 31), (1, 0, 25),
+    (3, 7, 0, 8), (1, 0, 26), (1, 2, 27), (1, 1, 31), (1, 0, 28), (1, 0, 29), (1, 2, 30), (3, 8, 0, 8),
+    (1, 1, 30), (1, 0, 30), (1, 0, 31), (3, 9, 0, 8),
 )
 
 

time: 46.4 us -> 46.1 us (level)
  no operation moved by 1% of the time
where the time goes in v4:
time: 46.1 us; the launch traced here: 46 us
  Pallas kernels  44.4 us (96%)
  local copies, waits for them, and re-layouts  1.6 us (3%)
    pallas_call x1, Pallas kernels, on_device(): pl.pallas_call(kernel, out_shape=jax.ShapeDtypeStruct((SEQ, 2, TILE // SE...  44.4 us
    reshape x1, local copies, waits for them, and re-layouts, on_device(): return jnp.transpose(out.reshape(2 * SEQ, TILE // SEQ, CH), (1, 0, 2))  1.6 us

profile of v4, /device:TPU:1, one launch (start us, length us, event | category | flops | bytes accessed | tf_op | source)
XLA Modules:
  0.0 46.0 jit_solution(12678414873390758873)
XLA Ops:
  0.0 44.4 %shard_map.64 = bf16[8,2,16,256]{3,2,1,0:T(8,128)(2,1)} custom-call(bf16[2,128,256]{2,1,0:T(8,128)(2,1)} %x_hbm.1, bf16[8,128,4096]{2,1,0:T(8,128)(2,1)} %bias_ref.1, s32[32,32]{1,0:T(8,128)} %filter_hbm.1, f32[1,256]{1,0:T(1,128)} %bitcast.6, bf16[256,1024]{1,0:T(8,128)(2,1)} %w_hbm.1, bf16[256,256]{1,0:T(8,128)(2,1)} %wf_hbm.1), custom_call_target="tpu_custom_call" | custom-call | flops 4294967296 | bytes 9437184 | tf_op jit(solution)/shard_map/pallas_call | solution.py:291
  44.4 1.6 %copy.9 = bf16[16,16,256]{2,0,1:T(8,128)(2,1)} copy(bf16[16,16,256]{2,1,0:T(8,128)(2,1)} %bitcast.5) | data formatting | bytes 262144 | tf_op jit(solution)/shard_map/reshape | solution.py:330

commit v5 on v4

--- a/solution.py
+++ b/solution.py
@@ -243,45 +243,41 @@
     advance(None)
     advance(None)
 
-    attended = []
-    for h in range(HEADS):
-        inverse = 1.0 / acc[h, 2 * DH : 2 * DH + 1, :]
-        attended.append(
-            jnp.concatenate(
-                [
-                    acc[h, 0:DH, 0:TILE] * inverse[:, 0:TILE],
-                    acc[h, DH : 2 * DH, TILE:] * inverse[:, TILE:],
-                ],
-                axis=1,
+    share = TILE // SEQ
+    sent, mine = [], []
+    for part in range(2):
+        lanes = slice(TILE * part, TILE * part + TILE)
+        attended = [
+            acc[h, DH * part : DH * part + DH, lanes] * (1.0 / acc[h, 2 * DH : 2 * DH + 1, lanes])
+            for h in range(HEADS)
+        ]
+        gated = (gate_ref[:, lanes] * jnp.concatenate(attended, axis=0)).astype(BF)
+        new = lax.dot_general(gated, wf_ref[...], TN, preferred_element_type=F32)
+        update[part] = new.astype(BF)
+
+        def share_of(owner):
+            return update.at[part, pl.ds(pl.multiple_of(owner * share, share), share)]
+
+        for k in (4, 3, 5, 2, 6, 1, 7):
+            owner = (seq + k) % SEQ
+            copy = pltpu.make_async_remote_copy(
+                src_ref=share_of(owner),
+                dst_ref=out_ref.at[seq, part],
+                send_sem=out_send.at[k, part],
+                recv_sem=out_recv.at[k, part],
+                device_id=(owner, res),
+                device_id_type=MESH,
             )
-        )
-    gated = (gate_ref[...] * jnp.concatenate(attended, axis=0)).astype(BF)
-    new = lax.dot_general(gated, wf_ref[...], TN, preferred_element_type=F32)
-    update[...] = new.astype(BF).reshape(2, TILE, CH)
-
-    share = TILE // SEQ
-
-    def share_of(owner):
-        return update.at[:, pl.ds(pl.multiple_of(owner * share, share), share)]
-
-    sent = []
-    for k in (4, 3, 5, 2, 6, 1, 7):
-        owner = (seq + k) % SEQ
-        copy = pltpu.make_async_remote_copy(
-            src_ref=share_of(owner),
-            dst_ref=out_ref.at[seq],
-            send_sem=out_send.at[k],
-            recv_sem=out_recv.at[k],
-            device_id=(owner, res),
-            device_id_type=MESH,
-        )
-        copy.start()
-        sent.append(copy)
-    mine = pltpu.make_async_copy(share_of(seq), out_ref.at[seq], out_recv.at[0])
-    mine.start()
+            copy.start()
+            sent.append(copy)
+        mine.append(
+            pltpu.make_async_copy(share_of(seq), out_ref.at[seq, part], out_recv.at[0, part])
+        )
+        mine[part].start()
     for copy in started:
         copy.wait_send()
-    mine.wait()
+    for copy in mine:
+        copy.wait()
     for copy in sent:
         copy.wait()
 
@@ -317,8 +313,8 @@
             pltpu.SemaphoreType.DMA((TILES, len(PARTS))),
             pltpu.SemaphoreType.DMA((TILES, len(PARTS))),
             pltpu.SemaphoreType.DMA((TILES,)),
-            pltpu.SemaphoreType.DMA((SEQ,)),
-            pltpu.SemaphoreType.DMA((SEQ,)),
+            pltpu.SemaphoreType.DMA((SEQ, 2)),
+            pltpu.SemaphoreType.DMA((SEQ, 2)),
         ],
         compiler_params=pltpu.CompilerParams(
             collective_id=0, has_side_effects=True, vmem_limit_bytes=63 * 2**20

time: 46.1 us -> 46.4 us (level)
  no operation moved by 1% of the time
where the time goes in v5:
time: 46.4 us; the launch traced here: 46.3 us
  Pallas kernels  44.7 us (96%)
  local copies, waits for them, and re-layouts  1.6 us (3%)
    pallas_call x1, Pallas kernels, on_device(): pl.pallas_call(kernel, out_shape=jax.ShapeDtypeStruct((SEQ, 2, TILE // SE...  44.7 us
    reshape x1, local copies, waits for them, and re-layouts, on_device(): return jnp.transpose(out.reshape(2 * SEQ, TILE // SEQ, CH), (1, 0, 2))  1.6 us

profile of v5, /device:TPU:1, one launch (start us, length us, event | category | flops | bytes accessed | tf_op | source)
XLA Modules:
  0.0 46.3 jit_solution(9619970328500293000)
XLA Ops:
  0.0 44.7 %shard_map.64 = bf16[8,2,16,256]{3,2,1,0:T(8,128)(2,1)} custom-call(bf16[2,128,256]{2,1,0:T(8,128)(2,1)} %x_hbm.1, bf16[8,128,4096]{2,1,0:T(8,128)(2,1)} %bias_ref.1, s32[32,32]{1,0:T(8,128)} %filter_hbm.1, f32[1,256]{1,0:T(1,128)} %bitcast.6, bf16[256,1024]{1,0:T(8,128)(2,1)} %w_hbm.1, bf16[256,256]{1,0:T(8,128)(2,1)} %wf_hbm.1), custom_call_target="tpu_custom_call" | custom-call | flops 4294967296 | bytes 9437184 | tf_op jit(solution)/shard_map/pallas_call | solution.py:287
  44.7 1.6 %copy.9 = bf16[16,16,256]{2,0,1:T(8,128)(2,1)} copy(bf16[16,16,256]{2,1,0:T(8,128)(2,1)} %bitcast.5) | data formatting | bytes 262144 | tf_op jit(solution)/shard_map/reshape | solution.py:326
